TPU v7x, 128 devices: a whole 4x4x4 slice. The times are simulated.
128 devices in a mesh: row: 8 (over z, y_lo), col: 16 (over y_hi, x, core).
Axes of the slice: x: 4, y: 4 (y_hi: 2, y_lo: 2; y = y_hi * 2 + y_lo), z: 4, core: 2. Of those that a mesh axis runs over, the one named last changes fastest.
Arguments:
- three_centre: bfloat16 [512, 64, 4096], P(('row', 'col')), may hold values from -6 to 6
- screen_mask: int32 [8, 64], replicated, may hold values 0 or 1
- block_counts: int32 [9], replicated, may hold values from 32 to 64, as said below
- green_occ: bfloat16 [512, 192], P('row'), may hold values from -0.4375 to 0.4375
- occ_mask: int32 [8, 3], replicated, may hold values 0 or 1
- green_virt: bfloat16 [64, 64], replicated, may hold values from -0.75 to 0.75
Outputs:
- chi: float32 [4096, 4096], P('col', 'row')
Inputs may be any that keep to these rules, and one draw needn't show every extreme that they name: `block_counts`: entry b < 8 counts the live functions of mu block b, entry 8 those of the nu block; live functions come first in a block.
All inputs are finite; a program needn't handle non-finite values.
Results may differ from a plain program's by a relative error of at most 0.013.
Values may be sent and summed in bfloat16 or wider, within the bound.
No kernel may reach another device: no remote copies, remote signals or barrier semaphores. Data moves between devices by JAX's collectives and lax.ppermute only.
A program may use at most 128 MiB of HBM per device.

v0:
```python
import math

import jax
import jax.numpy as jnp
from jax import lax
from jax.sharding import PartitionSpec as P


def extended(cells, sides, width):
    for axis, dim in sides:
        count = lax.axis_size(axis)
        head = lax.slice_in_dim(cells, 0, width, axis=dim)
        tail = lax.slice_in_dim(cells, cells.shape[dim] - width, cells.shape[dim], axis=dim)
        cells = jnp.concatenate(
            [
                lax.ppermute(tail, axis, [(i, (i + 1) % count) for i in range(count)]),
                cells,
                lax.ppermute(head, axis, [((i + 1) % count, i) for i in range(count)]),
            ],
            axis=dim,
        )
    return cells


def local(three_centre, screen_mask, block_counts, green_occ, occ_mask, green_virt):
    rows_total = lax.axis_size("row")
    cols_total = lax.axis_size("col")
    row_index = lax.axis_index("row")
    col_index = lax.axis_index("col")
    block_size = green_occ.shape[0]
    width_nu = three_centre.shape[1]
    slab_width = three_centre.shape[2]
    p_share = slab_width // cols_total
    chi_scale = -1.0 / math.sqrt(block_size * rows_total * width_nu)
    bf_zero = jnp.zeros((), jnp.bfloat16)
    count_mu = lax.dynamic_index_in_dim(block_counts, row_index, 0, keepdims=False)
    count_nu = block_counts[rows_total]
    nu_ok = jnp.arange(width_nu, dtype=jnp.int32) < count_nu
    p_row = (
        jnp.repeat(lax.dynamic_index_in_dim(screen_mask, row_index, 0, keepdims=False), block_size)
        > 0
    )
    exchanged = lax.all_to_all(three_centre, "col", split_axis=2, concat_axis=0, tiled=True)
    p_own = lax.dynamic_slice_in_dim(p_row, col_index * p_share, p_share, 0)
    mu_ok = jnp.arange(block_size, dtype=jnp.int32) < count_mu
    keep_mask = mu_ok[:, None, None] & nu_ok[None, :, None] & p_own[None, None, :]
    screened = jnp.where(keep_mask, exchanged, bf_zero)
    neighbours = extended(screened, (("row", 0),), block_size)
    band_mask = jnp.repeat(
        lax.dynamic_index_in_dim(occ_mask, row_index, 0, keepdims=False), block_size
    ).astype(jnp.bfloat16)
    occupied = jnp.dot(
        green_occ * band_mask[None, :],
        neighbours.reshape(3 * block_size, width_nu * p_share),
        preferred_element_type=jnp.float32,
    ).astype(jnp.bfloat16)
    virtual = jnp.einsum(
        "anp,nm->amp",
        occupied.reshape(block_size, width_nu, p_share),
        green_virt,
        preferred_element_type=jnp.float32,
    ).astype(jnp.bfloat16)
    pair_rows = virtual.reshape(block_size * width_nu, p_share)
    segment = lax.all_gather(screened, "col", axis=2, tiled=True)
    piece_cols = segment.shape[2]
    product = lax.dot_general(
        pair_rows,
        segment.reshape(block_size * width_nu, piece_cols),
        (((0,), (0,)), ((), ())),
        preferred_element_type=jnp.float32,
    )
    term = chi_scale * product
    return lax.psum_scatter(
        term.astype(jnp.bfloat16), "row", scatter_dimension=1, tiled=True
    ).astype(jnp.float32)


def solution(mesh):
    in_specs = (P(("row", "col"), None, None), P(), P(), P("row", None), P(), P())
    out_specs = P("col", "row")
    return jax.shard_map(local, mesh=mesh, in_specs=in_specs, out_specs=out_specs, check_vma=False)
```

profile of v0, /device:TPU:32, one launch (start us, length us, event | category | flops | bytes accessed | tf_op | source)
XLA Modules:
  0.0 407.7 jit_solution(6292827948399722791)
XLA Ops:
  6.5 6.9 %copy.8 = bf16[4,64,4096]{1,0,2:T(4,128)(2,1)} copy(bf16[4,64,4096]{2,1,0:T(8,128)(2,1)} %param.6) | data formatting | bytes 4194304 | tf_op args[0]
  13.5 7.5 %reshape.67 = bf16[16,2,32768]{2,1,0:T(2,128)(2,1)} reshape(bf16[4096,4,64]{2,1,0:T(4,128)(2,1)} %bitcast.34) | data formatting | bytes 4194304
  21.0 7.2 %all-to-all-start = ((bf16[16,2,32768]{2,1,0:T(2,128)(2,1)}), bf16[16,2,32768]{2,1,0:T(2,128)(2,1)S(1)}, u32[]{:S(2)}, u32[]{:S(2)}) async-start(bf16[16,2,32768]{2,1,0:T(2,128)(2,1)} %reshape.67), calls=%async_computation | async-start | bytes 4194304 | tf_op jit(solution)/shard_map/all_to_all | solution.py:43
  28.2 0.7 compare_bitcast_fusion
  29.2 0.7 fusion.11
  29.8 1.3 iota_compare_fusion
  31.2 26.2 %all-to-all-done = bf16[16,2,32768]{2,1,0:T(2,128)(2,1)S(1)} async-done(((bf16[16,2,32768]{2,1,0:T(2,128)(2,1)}), bf16[16,2,32768]{2,1,0:T(2,128)(2,1)S(1)}, u32[]{:S(2)}, u32[]{:S(2)}) %all-to-all-start) | async-done | bytes 2097184 | tf_op jit(solution)/shard_map/all_to_all | solution.py:43
  57.4 5.0 %reshape.68 = bf16[4096,4,64]{2,1,0:T(4,128)(2,1)} reshape(bf16[16,2,32768]{2,1,0:T(2,128)(2,1)S(1)} %all-to-all-done) | data formatting | bytes 4194304
  62.4 5.4 %copy.9 = bf16[4,64,16,256]{3,1,0,2:T(8,128)(2,1)S(1)} copy(bf16[4,64,16,256]{1,0,3,2:T(4,128)(2,1)} %bitcast.33) | data formatting | bytes 4194304 | tf_op jit(solution)/shard_map/all_to_all | solution.py:43
  67.7 2.1 and_select_fusion
  69.9 1.5 copy-done.1
  71.4 0.7 collective-permute-start
  72.0 2.2 collective-permute-start.1
  74.3 0.2 fusion.10
  74.6 68.7 %collective-permute-done = bf16[64,64,256]{2,1,0:T(8,128)(2,1)} collective-permute-done((bf16[64,64,256]{2,1,0:T(8,128)(2,1)S(1)}, bf16[64,64,256]{2,1,0:T(8,128)(2,1)}, u32[]{:S(2)}, u32[]{:S(2)}) %collective-permute-start) | collective-permute-done | bytes 2097184 | tf_op jit(solution)/shard_map/ppermute | solution.py:16
  143.4 78.2 %collective-permute-done.1 = bf16[64,64,256]{2,1,0:T(8,128)(2,1)} collective-permute-done((bf16[64,64,256]{2,1,0:T(8,128)(2,1)S(1)}, bf16[64,64,256]{2,1,0:T(8,128)(2,1)}, u32[]{:S(2)}, u32[]{:S(2)}) %collective-permute-start.1) | collective-permute-done | bytes 2097184 | tf_op jit(solution)/shard_map/ppermute | solution.py:18
  221.6 3.2 pad_maximum_fusion
  224.8 4.6 %copy.10 = bf16[24,8,64,256]{3,1,2,0:T(8,128)(2,1)S(1)} copy(bf16[24,8,64,256]{3,2,1,0:T(8,128)(2,1)S(1)} %bitcast.31) | data formatting | bytes 12582912
  229.4 1.3 convolution_convert_fusion
  230.7 0.5 copy.11
  231.2 100.5 %all-gather.2.cloned.1.call-done = bf16[64,64,4096]{2,1,0:T(8,128)(2,1)} async-done(((bf16[64,64,256]{2,1,0:T(8,128)(2,1)}), bf16[64,64,4096]{2,1,0:T(8,128)(2,1)}) %all-gather.2.cloned.1.call-update) | async-done | bytes 33554448 | tf_op jit(solution)/shard_map/all_gather | solution.py:64
  331.7 17.0 %fusion.1 = bf16[256,4096]{1,0:T(8,128)(2,1)} fusion(bf16[64,64,4096]{2,1,0:T(8,128)(2,1)} %all-gather.2.cloned.1.call-done, bf16[64,64,256]{2,1,0:T(8,128)(2,1)S(1)} %bitcast.35, bf16[64,64]{1,0:T(8,128)(2,1)S(1)} %copy-done), kind=kOutput, calls=%fused_computation.4 | convolution fusion | flops 8727298048 | bytes 37756928 | tf_op jit(solution)/shard_map/dot_general | solution.py:66
  348.7 50.3 %reduce-scatter.2.cloned.1.call-done = bf16[256,512]{1,0:T(8,128)(2,1)} async-done(((bf16[256,4096]{1,0:T(8,128)(2,1)}), bf16[256,512]{1,0:T(8,128)(2,1)}) %reduce-scatter.2.cloned.1.call-update) | async-done | bytes 262160 | tf_op jit(solution)/shard_map/reduce_scatter | solution.py:73
  399.1 1.8 convert_element_type.36
  (19 shorter events, 0.6 us)
Async XLA Ops:
  6.5 325.1 %copy-start = (bf16[64,64]{1,0:T(8,128)(2,1)S(1)}, bf16[64,64]{1,0:T(8,128)(2,1)}, u32[]{:S(2)}) copy-start(bf16[64,64]{1,0:T(8,128)(2,1)} %param.11) | copy-start | bytes 24580
  21.0 8.2 %copy-start.4 = (s32[9]{0:T(128)S(1)}, s32[9]{0:T(128)}, u32[]{:S(2)}) copy-start(s32[9]{0:T(128)} %param.8) | copy-start | bytes 112
  21.0 36.4 %all-to-all-start = ((bf16[16,2,32768]{2,1,0:T(2,128)(2,1)}), bf16[16,2,32768]{2,1,0:T(2,128)(2,1)S(1)}, u32[]{:S(2)}, u32[]{:S(2)}) async-start(bf16[16,2,32768]{2,1,0:T(2,128)(2,1)} %reshape.67), calls=%async_computation | async-start | bytes 4194304 | tf_op jit(solution)/shard_map/all_to_all | solution.py:43
  28.2 303.5 %all-gather.2.cloned.1.call-start = ((), (), s32[]{:S(2)}) async-start(), calls=%async_computation.2 | async-start | bytes 35651584 | tf_op jit(solution)/shard_map/all_gather | solution.py:64
  69.8 1.6 copy-start.1
  69.8 4.5 %copy-start.3 = (s32[8,3]{0,1:T(4,128)S(1)}, s32[8,3]{0,1:T(4,128)}, u32[]{:S(2)}) copy-start(s32[8,3]{0,1:T(4,128)} %param.10) | copy-start | bytes 292
  69.8 329.3 %reduce-scatter.2.cloned.1.call-start = ((), (), s32[]{:S(2)}) async-start(), calls=%async_computation.3 | async-start | bytes 2359296 | tf_op jit(solution)/shard_map/reduce_scatter | solution.py:73
  71.4 72.0 %collective-permute-start = (bf16[64,64,256]{2,1,0:T(8,128)(2,1)S(1)}, bf16[64,64,256]{2,1,0:T(8,128)(2,1)}, u32[]{:S(2)}, u32[]{:S(2)}) collective-permute-start(bf16[64,64,256]{2,1,0:T(8,128)(2,1)S(1)} %copy-done.1), channel_id=1, source_target_pairs={{0,16},{16,32},{32,48},{48,64},{64,80},{80,96},{96,112},{112,0},{1... | collective-permute-start | bytes 6291464 | tf_op jit(solution)/shard_map/ppermute | solution.py:16
  72.0 149.5 %collective-permute-start.1 = (bf16[64,64,256]{2,1,0:T(8,128)(2,1)S(1)}, bf16[64,64,256]{2,1,0:T(8,128)(2,1)}, u32[]{:S(2)}, u32[]{:S(2)}) collective-permute-start(bf16[64,64,256]{2,1,0:T(8,128)(2,1)S(1)} %copy-done.1), channel_id=1, source_target_pairs={{16,0},{32,16},{48,32},{64,48},{80,64},{96,80},{112,96},{0,112},{1... | collective-permute-start | bytes 6291464 | tf_op jit(solution)/shard_map/ppermute | solution.py:18
  224.8 4.6 %copy-start.2 = (bf16[64,192]{1,0:T(8,128)(2,1)S(1)}, bf16[64,192]{1,0:T(8,128)(2,1)}, u32[]{:S(2)}) copy-start(bf16[64,192]{1,0:T(8,128)(2,1)} %param.9) | copy-start | bytes 73732
Sparse Core Ops, SparseCore 0:
  69.9 261.7 all-gather.1
  348.9 50.1 reduce-scatter.1
where the time goes:
time: 411 us; the launch traced here: 408 us
  waiting for transfers between devices  324 us (79%)
  local copies, waits for them, and re-layouts  32.5 us (8%)
  matrix products  18.3 us (4%)
  between operations  13.5 us (3%)
  starting transfers between devices  10.2 us (2%)
  other arithmetic  9.3 us (2%)
    all_gather x1, waiting for transfers between devices, local(): segment = lax.all_gather(screened, 'col', axis=2, tiled=True)  100 us
    ppermute x1, waiting for transfers between devices, extended(): lax.ppermute(head, axis, [((i + 1) % count, i) for i in range(count)])  78.2 us
    ppermute x1, waiting for transfers between devices, extended(): lax.ppermute(tail, axis, [(i, (i + 1) % count) for i in range(count)])  68.7 us
    reduce_scatter x1, waiting for transfers between devices, local(): lax.psum_scatter(term.astype(jnp.bfloat16), 'row', scatter_dimension=1, t...  50.3 us
    all_to_all x1, waiting for transfers between devices, local(): lax.all_to_all(three_centre, 'col', split_axis=2, concat_axis=0, tiled=True)  26.2 us
    unnamed x15, local copies, waits for them, and re-layouts  26 us
    dot_general x1, matrix products, local(): lax.dot_general(pair_rows, segment.reshape(block_size * width_nu, piece_c...  17 us
  transfers between devices with their start and end apart: 5, of which 5 were waited for; matrix products, arithmetic and copies ran while one was open for 3% of the time, Pallas kernels for 0%

commit v1 on v0

v1 whole, which is shorter than its diff:
```python
import functools
import math

import jax
import jax.numpy as jnp
from jax import lax
from jax.experimental import pallas as pl
from jax.experimental.pallas import tpu as pltpu
from jax.sharding import Mesh, PartitionSpec as P

AXES = ("zhi", "zlo", "ylo", "yhi", "x", "core")
SIZES = (2, 2, 2, 2, 4, 2)
ROWS = ("zhi", "zlo", "ylo")
COLS = ("yhi", "x", "core")
GROUP = ("zlo", "ylo", "x")
BS = 64
NU = 64
NB = 8
NG = 16
MUD = 4
SRC = 16
PSL = 4096
W = 256
LINES = 8
TAIL = 128
WIDE = 4 * W
BF = jnp.bfloat16
F32 = jnp.float32
SCALE = -1.0 / math.sqrt(NB * BS * NU)
PARAMS = pltpu.CompilerParams(vmem_limit_bytes=48 * 1024 * 1024)


def iota(shape, axis):
    return lax.broadcasted_iota(jnp.int32, shape, axis)


def cost(flops, size):
    return pl.CostEstimate(flops=flops, bytes_accessed=size, transcendentals=0)


def in_hbm(value):
    return pltpu.with_memory_space_constraint(value, pltpu.HBM)


def pack_kernel(per, part, rows, pos_ref, screen_ref, counts_ref, gv_ref, *refs):
    (x0, x1, x2, x3), out_ref, lhs = refs[:4], refs[-2], refs[-1]
    step = pl.program_id(0)
    row = pos_ref[0]
    col = pos_ref[1]
    full = NG * rows

    @pl.when(step == 0)
    def _():
        def place(shape):
            line = iota(shape, 0)
            group, r = line // rows, line % rows
            if part == 0:
                plain = r >= MUD * per
                mu = jnp.where(plain, r - MUD * per, r // per)
                j = jnp.where(plain, per - 1, r % per)
            else:
                width = rows // MUD
                plain = r >= 0
                mu = r // width
                j = r % width
            return plain, mu, group * per + j

        plain, _, m = place((full, NU))
        pick = (m == iota((full, NU), 1)).astype(F32)
        if part == 0:
            gv_t = gv_ref[...].astype(F32).T
            small = jnp.dot(pick, gv_t, preferred_element_type=F32)
            small = jnp.where(plain, pick, small)
        else:
            small = pick
        big = jnp.concatenate([small] * MUD, axis=1)
        _, mu, _ = place((full, MUD * NU))
        lane = iota((full, MUD * NU), 1)
        live = (
            (mu == lane // NU)
            & (lane % NU < counts_ref[NB])
            & (mu + MUD * col < counts_ref[row])
        )
        lhs[...] = jnp.where(live, big, 0.0).astype(BF)

    half, core = step // 2, step % 2
    sub = iota((1, W), 1) // BS

    def store(g, lanes, piece):
        zlo, ylo, xx = g // 8, (g // 4) % 2, g % 4
        for copy in range(2):
            if part == 0:
                out_ref[copy, zlo, ylo, xx, :, lanes] = piece
            else:
                out_ref[zlo, ylo, copy, xx, :, lanes] = piece

    for t, ref in enumerate((x0, x1, x2, x3)):
        mask = jnp.zeros((1, W), F32)
        for k in range(W // BS):
            on = screen_ref[row, (half * 8 + 2 * t + core) * (W // BS) + k] > 0
            mask = jnp.where(sub == k, on.astype(F32), mask)
        cells = ref[...].reshape(MUD * NU, W)
        out = jnp.dot(lhs[...], cells, preferred_element_type=F32) * mask
        for g in range(NG):
            piece = out[g * rows : (g + 1) * rows]
            if part == 0:
                for h in range(rows // LINES):
                    at = h * WIDE + t * W
                    store(g, slice(at, at + W), piece[h * LINES : (h + 1) * LINES].astype(BF))
            else:
                store(g, slice(t * W, (t + 1) * W), piece.astype(BF))
    if part == 0:
        green = refs[4][...]
        line, mu = iota((LINES, BS), 0), iota((LINES, BS), 1)
        left = (mu == MUD * col + line).astype(BF)
        right = (mu == MUD * col + line - MUD).astype(BF)
        left = jnp.where(line < MUD, left, jnp.zeros_like(left))
        right = jnp.where(line < MUD, jnp.zeros_like(right), right)
        tail = jnp.dot(left, green[:, :TAIL], preferred_element_type=F32)
        low = jnp.dot(right, green[:, TAIL:], preferred_element_type=F32)
        tail = (tail + jnp.concatenate([low, jnp.zeros_like(low)], axis=1)).astype(BF)
        at = rows // LINES * WIDE
        for g in range(NG):
            store(g, slice(at, at + TAIL), tail)


def pack(per, part, rows, pos, screen_mask, counts, green_virt, green_occ, cells):
    if part == 0:
        shape = (LINES, rows // LINES * WIDE + TAIL)
        block = (2, 2, 2, None, 4, None) + shape
        index = lambda s, *_: (0, 0, 0, s // 2, 0, s % 2, 0, 0)
    else:
        shape = (rows, WIDE)
        block = (None, 2, 2, 2, 4, None) + shape
        index = lambda s, *_: (s // 2, 0, 0, 0, 0, s % 2, 0, 0)

    def column(t):
        return pl.BlockSpec((MUD, NU, W), lambda s, *_: (0, 0, (s // 2) * 8 + 2 * t + s % 2))

    operands = [green_virt] + [cells] * 4
    in_specs = [pl.BlockSpec((NU, NU), lambda s, *_: (0, 0))] + [column(t) for t in range(4)]
    if part == 0:
        operands.append(green_occ)
        in_specs.append(pl.BlockSpec((BS, 3 * BS), lambda s, *_: (0, 0)))
    out = pl.pallas_call(
        functools.partial(pack_kernel, per, part, rows),
        grid_spec=pltpu.PrefetchScalarGridSpec(
            num_scalar_prefetch=3,
            grid=(4,),
            in_specs=in_specs,
            out_specs=pl.BlockSpec(block, index),
            scratch_shapes=[pltpu.VMEM((NG * rows, MUD * NU), BF)],
        ),
        out_shape=pltpu.HBM(SIZES + shape, BF),
        compiler_params=PARAMS,
        cost_estimate=cost(2 * NG * rows * 256 * PSL, 6 << 20),
        name=f"pack_{part}",
    )(pos, screen_mask, counts, *operands)
    return out.reshape((128,) + shape)


def band_kernel(per, mask_ref, c0, c1, c2, c3, *out_refs):
    step = pl.program_id(0)
    refs = (c0, c1, c2, c3)
    lines = SRC * LINES
    halves = c0.shape[1] // WIDE
    depth = lines * halves
    width = 2 if per == 3 else per
    main = BS * width
    count = BS * per

    def place_row(shape):
        line = iota(shape, 0)
        extra = line >= main
        return jnp.where(extra, line - main, line // width), jnp.where(extra, width, line % width)

    def place_col(shape):
        line = iota(shape, 1)
        half, line = line // lines, line % lines
        source, r = line // LINES, line % LINES + half * LINES
        return r < MUD * per, source * MUD + r // per, r % per

    row_mu, _ = place_row((count, BS))
    spread_rows = (row_mu == iota((count, BS), 1)).astype(BF)
    good, col_mu, _ = place_col((BS, depth))
    spread_cols = (good & (col_mu == iota((BS, depth), 0))).astype(BF)
    _, row_j = place_row((count, depth))
    _, _, col_j = place_col((count, depth))
    same = row_j == col_j
    line, at = iota((BS, lines), 0), iota((BS, lines), 1)
    spot = (line // MUD) * LINES + line % MUD
    take_left = (spot == at).astype(BF)
    take_right = (spot + MUD == at).astype(BF)
    blocks = [
        jnp.concatenate([ref[:, h * WIDE : (h + 1) * WIDE] for h in range(halves)], axis=0)
        for ref in refs
    ]
    mains, extras = [], []
    for u in range(2):
        total = jnp.zeros((count, WIDE), F32)
        packed = refs[u + 1][:, halves * WIDE :]
        left = jnp.dot(take_left, packed, preferred_element_type=F32).astype(BF)
        right = jnp.dot(take_right, packed, preferred_element_type=F32).astype(BF)
        left = jnp.dot(spread_rows, left, preferred_element_type=F32).astype(BF)
        right = jnp.dot(spread_rows, right, preferred_element_type=F32).astype(BF)
        for k, part in enumerate((left[:, :BS], left[:, BS:], right[:, :BS])):
            part = jnp.dot(part, spread_cols, preferred_element_type=F32)
            part = jnp.where(same, part * mask_ref[2 * step + u, k].astype(F32), 0.0).astype(BF)
            total += jnp.dot(part, blocks[u + k], preferred_element_type=F32)
        mains.append(total[:main])
        extras.append(total[main:])
        if per == 3:
            line, at = iota((BS, lines), 0), iota((BS, lines), 1)
            take = ((line // MUD) * LINES + MUD + line % MUD == at).astype(BF)
            out_refs[2][u * BS : (u + 1) * BS, :] = jnp.dot(
                take, blocks[u + 1][lines:], preferred_element_type=F32
            ).astype(BF)
    out_refs[0][...] = jnp.concatenate(mains, axis=0).astype(BF).T
    if per == 3:
        out_refs[1][...] = jnp.concatenate(extras, axis=0).astype(BF).T


def band(per, occ_mask, cells):
    lines, full = SRC * LINES, cells.shape[1]
    width = 2 if per == 3 else per
    blk = lambda off: pl.BlockSpec((lines, full), lambda s, *_: ((2 * s + off) % NB, 0))
    out_specs = [pl.BlockSpec((WIDE, 2 * BS * width), lambda s, *_: (0, s))]
    out_shape = [jax.ShapeDtypeStruct((WIDE, NB * BS * width), BF)]
    if per == 3:
        out_specs.append(pl.BlockSpec((WIDE, 2 * BS), lambda s, *_: (0, s)))
        out_shape.append(jax.ShapeDtypeStruct((WIDE, NB * BS), BF))
        out_specs.append(pl.BlockSpec((2 * BS, WIDE), lambda s, *_: (s, 0)))
        out_shape.append(pltpu.HBM((NB * BS, WIDE), BF))
    return pl.pallas_call(
        functools.partial(band_kernel, per),
        grid_spec=pltpu.PrefetchScalarGridSpec(
            num_scalar_prefetch=1,
            grid=(NB // 2,),
            in_specs=[blk(off) for off in (NB - 1, 0, 1, 2)],
            out_specs=out_specs,
        ),
        out_shape=out_shape,
        compiler_params=PARAMS,
        cost_estimate=cost(2 * NB * BS * per * 3 * full // WIDE * lines * WIDE, 12 << 20),
        name="band",
    )(occ_mask, cells, cells, cells, cells)


def product_kernel(pairs, pos_ref, *refs):
    out = jnp.dot(refs[0][...], refs[1][...], preferred_element_type=F32)
    for i in range(1, pairs):
        out += jnp.dot(refs[2 * i][...], refs[2 * i + 1][...], preferred_element_type=F32)
    out = (out * SCALE).astype(BF)
    for x in range(4):
        refs[-1][x] = out[x * W : (x + 1) * W]


def product(pos, virts, cells, before=None):
    operands, in_specs, flops = [], [], 0
    for virt, cell in zip(virts, cells):
        depth = cell.shape[0]
        operands += [virt, cell]
        in_specs += [
            pl.BlockSpec((WIDE, depth), lambda i, *_: (0, 0)),
            pl.BlockSpec((depth, W), lambda i, *_: (0, i)),
        ]
        flops += 2 * depth * WIDE * WIDE
    if before is None:
        index = lambda i, pos_ref: (i, 0, 0, pos_ref[2])
        alias = {}
    else:
        operands.append(before)
        in_specs.append(pl.BlockSpec(memory_space=pl.ANY))
        index = lambda i, pos_ref: (i, 0, 0, 1 - pos_ref[2])
        alias = {len(operands): 0}
    return pl.pallas_call(
        functools.partial(product_kernel, len(virts)),
        grid_spec=pltpu.PrefetchScalarGridSpec(
            num_scalar_prefetch=1,
            grid=(4,),
            in_specs=in_specs,
            out_specs=pl.BlockSpec((None, 4, W, W), index),
        ),
        out_shape=pltpu.HBM((4, 4, W, 2 * W), BF),
        input_output_aliases=alias,
        compiler_params=PARAMS,
        cost_estimate=cost(flops, 10 << 20),
        name="product",
    )(pos, *operands)


def total_kernel(ref, out_ref):
    acc = ref[0].astype(F32)
    for k in range(1, NG):
        acc += ref[k].astype(F32)
    out_ref[...] = acc


def total(value):
    tile = 64
    return pl.pallas_call(
        total_kernel,
        grid=(W // tile,),
        in_specs=[pl.BlockSpec((NG, tile, 2 * W), lambda i: (0, i, 0))],
        out_specs=pl.BlockSpec((tile, 2 * W), lambda i: (i, 0)),
        out_shape=jax.ShapeDtypeStruct((W, 2 * W), F32),
        compiler_params=PARAMS,
        cost_estimate=cost(2 << 20, 5 << 20),
        name="total",
    )(value)


def exchange(value, axes):
    return lax.all_to_all(value, axes, split_axis=0, concat_axis=0, tiled=True)


def run(per, pos, cells, screen_mask, counts, green_occ, occ_mask, green_virt):
    rows = (8 if per == 2 else 16, 16 if per == 4 else 8)
    first = pack(per, 0, rows[0], pos, screen_mask, counts, green_virt, green_occ, cells)
    second = pack(per, 1, rows[1], pos, screen_mask, counts, green_virt, green_occ, cells)
    first = exchange(first, AXES)
    second, first = lax.optimization_barrier((second, first))
    second = exchange(second, AXES).reshape(128 * rows[1], WIDE)
    outs = band(per, occ_mask, first.reshape(128 * LINES, first.shape[-1]))
    second, outs = lax.optimization_barrier((second, outs))
    virts = outs[:2]
    own = [second] + list(outs[2:])
    other = [lax.ppermute(v, "core", [(0, 1), (1, 0)]) for v in own]
    part = product(pos, virts, own)
    part = product(pos, virts, other, part)
    return total(exchange(part.reshape(NG, W, 2 * W), GROUP))


def local(three_centre, screen_mask, block_counts, green_occ, occ_mask, green_virt):
    row = lax.axis_index(ROWS)
    col = lax.axis_index(COLS)
    pos = jnp.stack([row, col, lax.axis_index("core")]).astype(jnp.int32)
    return run(
        4, pos, in_hbm(three_centre), screen_mask, block_counts, green_occ, occ_mask, in_hbm(green_virt)
    )


def solution(mesh):
    fine = Mesh(mesh.devices.reshape(SIZES), AXES)
    in_specs = (P(ROWS + COLS, None, None), P(), P(), P(ROWS, None), P(), P())
    return jax.shard_map(
        local, mesh=fine, in_specs=in_specs, out_specs=P(COLS, ROWS), check_vma=False
    )
```

time: 411 us -> 212 us (0.52)
  waiting for transfers between devices: 324 us -> 83.3 us
  blocking collectives: 0 us -> 57.3 us
  Pallas kernels: 0 us -> 41.3 us
  local copies, waits for them, and re-layouts: 32.5 us -> 8.29 us
  matrix products: 18.3 us -> 0 us
  between operations: 13.5 us -> 0.07 us
  other arithmetic: 9.3 us -> 0.08 us
  starting transfers between devices: 10.2 us -> 18.9 us
    ppermute x2 -> x1, waiting for transfers between devices: 147 us -> 0.01 us  [run(): other = [lax.ppermute(v, 'core', [(0, 1), (1, 0)]) for v in own]]
    all_gather x1 -> x0, waiting for transfers between devices: 100 us -> none  [local(): segment = lax.all_gather(screened, 'col', axis=2, tiled=True)]
    all_to_all x0 -> x1, blocking collectives: none -> 57.3 us  [exchange(): return lax.all_to_all(value, axes, split_axis=0, concat_axis=0, tiled=True)]
    all_to_all x1 -> x2, waiting for transfers between devices: 26.2 us -> 83.3 us  [exchange(): return lax.all_to_all(value, axes, split_axis=0, concat_axis=0, tiled=True)]
    reduce_scatter x1 -> x0, waiting for transfers between devices: 50.3 us -> none  [local(): lax.psum_scatter(term.astype(jnp.bfloat16), 'row', scatter_dimension=1, t...]
    pallas_call x0 -> x6, Pallas kernels: none -> 41.3 us  [the longest x2 15.6 us: product(): pl.pallas_call(functools.partial(product_kernel, len(virts)), grid_spec=p...]
    dot_general x2 -> x0, matrix products: 18.3 us -> none  [the longest x1 17 us: local(): lax.dot_general(pair_rows, segment.reshape(block_size * width_nu, piece_c...]
    unnamed x15 -> x19, local copies, waits for them, and re-layouts: 26 us -> 8.29 us
  transfers between devices with their start and end apart: 5 -> 3, of which waited for: 5 -> 2; matrix products, arithmetic and copies ran while one was open for 3% -> 0% of each run, Pallas kernels for 0% -> 12%
where the time goes in v1:
time: 212 us; the launch traced here: 209 us
  waiting for transfers between devices  83.3 us (39%)
  blocking collectives  57.3 us (27%)
  Pallas kernels  41.3 us (19%)
  starting transfers between devices  18.9 us (9%)
  local copies, waits for them, and re-layouts  8.29 us (4%)
    all_to_all x2, waiting for transfers between devices, exchange(): return lax.all_to_all(value, axes, split_axis=0, concat_axis=0, tiled=True)  83.3 us
    all_to_all x1, blocking collectives, exchange(): return lax.all_to_all(value, axes, split_axis=0, concat_axis=0, tiled=True)  57.3 us
    all_to_all x2, starting transfers between devices, exchange(): return lax.all_to_all(value, axes, split_axis=0, concat_axis=0, tiled=True)  18.9 us
    pallas_call x2, Pallas kernels, product(): pl.pallas_call(functools.partial(product_kernel, len(virts)), grid_spec=p...  15.6 us
    pallas_call x1, Pallas kernels, band(): pl.pallas_call(functools.partial(band_kernel, per), grid_spec=pltpu.Prefe...  12.1 us
    pallas_call x2, Pallas kernels, pack(): pl.pallas_call(functools.partial(pack_kernel, per, part, rows), grid_spec...  11.6 us
    unnamed x19, local copies, waits for them, and re-layouts  8.29 us
  transfers between devices with their start and end apart: 3, of which 2 were waited for; matrix products, arithmetic and copies ran while one was open for 0% of the time, Pallas kernels for 12%

profile of v1, /device:TPU:32, one launch (start us, length us, event | category | flops | bytes accessed | tf_op | source)
XLA Modules:
  0.0 209.2 jit_solution(13348614935978704988)
XLA Ops:
  0.0 0.1 pad_add_fusion.pos_ref
  0.1 0.8 copy-done.2
  0.8 0.7 copy-done.3
  1.5 0.7 copy-done.5
  2.2 5.9 %pack_0.1 = bf16[2,2,2,2,4,2,8,2176]{7,6,5,4,3,2,1,0:T(8,128)(2,1)} custom-call(s32[3]{0:T(128)S(1)} %pad_add_fusion.pos_ref, s32[8,64]{1,0:T(8,128)S(1)} %copy-done.3, s32[9]{0:T(128)S(1)} %copy-done.5, bf16[64,64]{1,0:T(8,128)(2,1)} %gv_ref.3, bf16[4,64,4096]{2,1,0:T(8,128)(2,1)} %refs_3_.3, bf16[4,64,4096]{2,1,0:T(8,128)(2,1)} %refs_3_.3, ...), custom_call_target="tpu_custom_call" | custom-call | flops 536870912 | bytes 6291456 | tf_op jit(solution)/shard_map/pack_0/pallas_call | solution.py:145
  8.1 10.6 %all-to-all-start = ((bf16[128,8,2176]{2,1,0:T(8,128)(2,1)}), bf16[128,8,2176]{2,1,0:T(8,128)(2,1)}, u32[]{:S(2)}, u32[]{:S(2)}) async-start(bf16[128,8,2176]{2,1,0:T(8,128)(2,1)} %bitcast.8), calls=%async_computation | async-start | bytes 8912896 | tf_op jit(solution)/shard_map/all_to_all | solution.py:314
  18.8 0.0 copy-done.4
  18.8 0.0 copy-done.6
  18.8 5.7 %pack_1.1 = bf16[2,2,2,2,4,2,16,1024]{7,6,5,4,3,2,1,0:T(8,128)(2,1)} custom-call(s32[3]{0:T(128)S(1)} %pad_add_fusion.pos_ref, s32[8,64]{1,0:T(8,128)S(1)} %copy-done.4, s32[9]{0:T(128)S(1)} %copy-done.6, bf16[64,64]{1,0:T(8,128)(2,1)} %gv_ref.3, bf16[4,64,4096]{2,1,0:T(8,128)(2,1)} %refs_3_.3, bf16[4,64,4096]{2,1,0:T(8,128)(2,1)} %refs_3_.3, ...), custom_call_target="tpu_custom_call" | custom-call | flops 536870912 | bytes 6291456 | tf_op jit(solution)/shard_map/pack_1/pallas_call | solution.py:145
  24.5 47.3 %all-to-all-done = bf16[128,8,2176]{2,1,0:T(8,128)(2,1)} async-done(((bf16[128,8,2176]{2,1,0:T(8,128)(2,1)}), bf16[128,8,2176]{2,1,0:T(8,128)(2,1)}, u32[]{:S(2)}, u32[]{:S(2)}) %all-to-all-start) | async-done | bytes 4456480 | tf_op jit(solution)/shard_map/all_to_all | solution.py:314
  71.8 8.3 %all-to-all-start.1 = ((bf16[128,16,1024]{2,1,0:T(8,128)(2,1)}), bf16[128,16,1024]{2,1,0:T(8,128)(2,1)}, u32[]{:S(2)}, u32[]{:S(2)}) async-start(bf16[128,16,1024]{2,1,0:T(8,128)(2,1)} %bitcast.9), calls=%async_computation.1 | async-start | bytes 8388608 | tf_op jit(solution)/shard_map/all_to_all | solution.py:314
  80.0 0.0 copy-done.8
  80.0 0.1 copy.8.mask_ref
  80.1 12.1 %band.1.refs_0_ = bf16[1024,2048]{1,0:T(8,128)(2,1)S(1)} custom-call(s32[8,3]{1,0:T(8,128)S(1)} %copy.8.mask_ref, bf16[1024,2176]{1,0:T(8,128)(2,1)} %bitcast.6.c0.c1.c2.c3, bf16[1024,2176]{1,0:T(8,128)(2,1)} %bitcast.6.c0.c1.c2.c3, bf16[1024,2176]{1,0:T(8,128)(2,1)} %bitcast.6.c0.c1.c2.c3, bf16[1024,2176]{1,0:T(8,128)(2,1)} %bitcast.6.c0.c1.c2.c3), custom_call_target="tpu_custom_call" | custom-call | flops 3422552064 | bytes 12582912 | tf_op jit(solution)/shard_map/band/pallas_call | solution.py:234
  92.2 1.9 copy-done
  94.1 36.1 %all-to-all-done.1 = bf16[128,16,1024]{2,1,0:T(8,128)(2,1)} async-done(((bf16[128,16,1024]{2,1,0:T(8,128)(2,1)}), bf16[128,16,1024]{2,1,0:T(8,128)(2,1)}, u32[]{:S(2)}, u32[]{:S(2)}) %all-to-all-start.1) | async-done | bytes 4194336 | tf_op jit(solution)/shard_map/all_to_all | solution.py:314
  130.2 0.0 collective-permute-start
  130.2 2.2 %copy-done.1 = bf16[1024,2048]{1,0:T(8,128)(2,1)S(1)} copy-done((bf16[1024,2048]{1,0:T(8,128)(2,1)S(1)}, bf16[1024,2048]{1,0:T(8,128)(2,1)}, u32[]{:S(2)}) %copy-start.1) | copy-done | bytes 4194328
  132.4 7.8 %product.2.refs_2_ = bf16[4,4,256,512]{3,2,1,0:T(8,128)(2,1)} custom-call(s32[3]{0:T(128)S(1)} %pad_add_fusion.pos_ref, bf16[1024,2048]{1,0:T(8,128)(2,1)S(1)} %copy-done.1, bf16[2048,1024]{1,0:T(8,128)(2,1)} %bitcast.5.refs_1_), custom_call_target="tpu_custom_call" | custom-call | flops 4294967296 | bytes 10485760 | tf_op jit(solution)/shard_map/product/pallas_call | solution.py:276
  140.2 0.0 collective-permute-done.refs_1_
  140.2 2.0 copy-done.7
  142.2 7.8 %product.3 = bf16[4,4,256,512]{3,2,1,0:T(8,128)(2,1)} custom-call(s32[3]{0:T(128)S(1)} %pad_add_fusion.pos_ref, bf16[1024,2048]{1,0:T(8,128)(2,1)S(1)} %copy-done.1, bf16[2048,1024]{1,0:T(8,128)(2,1)} %copy-done.7, bf16[4,4,256,512]{3,2,1,0:T(8,128)(2,1)} %product.2.refs_2_), custom_call_target="tpu_custom_call", output_to_operand_aliasing={{}: (3, {})} | custom-call | flops 4294967296 | bytes 10485760 | tf_op jit(solution)/shard_map/product/pallas_call | solution.py:276
  150.0 57.3 %all_to_all.15.ref = bf16[16,256,512]{2,1,0:T(8,128)(2,1)S(1)} all-to-all(bf16[16,256,512]{2,1,0:T(8,128)(2,1)} %bitcast.10), channel_id=1, replica_groups=mesh['zhi'=2,'zlo'=2,'ylo'=2,'yhi'=2,'x'=4,'core'=2] {'zlo','ylo','x'}, dimensions={0} | all-to-all | bytes 8388608 | tf_op jit(solution)/shard_map/all_to_all | solution.py:314
  207.3 2.0 total.1
  (9 shorter events, 0.0 us)
Async XLA Ops:
  0.1 0.8 copy-start.2
  0.8 0.7 copy-start.3
  1.5 0.7 copy-start.5
  8.1 10.6 %copy-start.4 = (s32[8,64]{1,0:T(8,128)S(1)}, s32[8,64]{1,0:T(8,128)}, u32[]{:S(2)}) copy-start(s32[8,64]{1,0:T(8,128)} %screen_ref.3) | copy-start | bytes 6148
  8.1 10.7 %copy-start.6 = (s32[9]{0:T(128)S(1)}, s32[9]{0:T(128)}, u32[]{:S(2)}) copy-start(s32[9]{0:T(128)} %counts_ref.3) | copy-start | bytes 112
  8.1 63.6 %all-to-all-start = ((bf16[128,8,2176]{2,1,0:T(8,128)(2,1)}), bf16[128,8,2176]{2,1,0:T(8,128)(2,1)}, u32[]{:S(2)}, u32[]{:S(2)}) async-start(bf16[128,8,2176]{2,1,0:T(8,128)(2,1)} %bitcast.8), calls=%async_computation | async-start | bytes 8912896 | tf_op jit(solution)/shard_map/all_to_all | solution.py:314
  71.8 8.3 %copy-start.8 = (s32[8,3]{0,1:T(4,128)S(1)}, s32[8,3]{0,1:T(4,128)}, u32[]{:S(2)}) copy-start(s32[8,3]{0,1:T(4,128)} %param.10) | copy-start | bytes 292
  71.8 58.4 %all-to-all-start.1 = ((bf16[128,16,1024]{2,1,0:T(8,128)(2,1)}), bf16[128,16,1024]{2,1,0:T(8,128)(2,1)}, u32[]{:S(2)}, u32[]{:S(2)}) async-start(bf16[128,16,1024]{2,1,0:T(8,128)(2,1)} %bitcast.9), calls=%async_computation.1 | async-start | bytes 8388608 | tf_op jit(solution)/shard_map/all_to_all | solution.py:314
  92.2 1.9 copy-start
  130.2 10.0 %collective-permute-start = (bf16[2048,1024]{1,0:T(8,128)(2,1)}, bf16[2048,1024]{1,0:T(8,128)(2,1)S(1)}, u32[]{:S(2)}, u32[]{:S(2)}) collective-permute-start(bf16[2048,1024]{1,0:T(8,128)(2,1)} %bitcast.5.refs_1_), channel_id=1, source_target_pairs={{0,1},{1,0},{2,3},{3,2},{4,5},{5,4},{6,7},{7,6},{8,9},{9,8},{10,11... | collective-permute-start | bytes 12582920 | tf_op jit(solution)/shard_map/ppermute | solution.py:328
  130.2 2.2 %copy-start.1 = (bf16[1024,2048]{1,0:T(8,128)(2,1)S(1)}, bf16[1024,2048]{1,0:T(8,128)(2,1)}, u32[]{:S(2)}) copy-start(bf16[1024,2048]{1,0:T(8,128)(2,1)} %copy-done) | copy-start | bytes 12582916
  140.2 2.0 copy-start.7
